TPU v7x, 512 devices: a whole 4x8x8 slice. The times are simulated.
512 devices in a mesh: ia: 16 (over z_lo, x, core), ja: 8 (over y), ka: 4 (over z_hi).
Axes of the slice: x: 4, y: 8, z: 8 (z_hi: 4, z_lo: 2; z = z_hi * 2 + z_lo), core: 2. Of those that a mesh axis runs over, the one named last changes fastest.
Arguments:
- tensor: float32 [512, 1024, 512], P('ia', 'ja', 'ka'), may hold values from -200 to 200
- factor_b: float32 [1024, 4, 96], P(('ja', 'ka')), may hold values from -4 to 4
- factor_c: float32 [512, 4, 96], P(('ka', 'ja')), may hold values from -4 to 4
Outputs:
- factor_a: float32 [512, 4, 96], P(('ia', 'ja', 'ka'))
- weights: float32 [4, 96], replicated
All inputs are finite; a program needn't handle non-finite values.
Results may differ from a plain program's by a relative error of at most 0.0003.
Values sent between devices are 32-bit elements; how exact they have to be, the bound alone decides.
No kernel may reach another device: no remote copies, remote signals or barrier semaphores. Data moves between devices by JAX's collectives and lax.ppermute only.
A program may use at most 64 MiB of HBM per device.

v0:
```python
import jax
import jax.numpy as jnp
from jax import lax
from jax.sharding import PartitionSpec as P

highest = lax.Precision.HIGHEST


def gram_of(rows):
    return jnp.einsum(
        "jsr,jsq->srq", rows, rows, precision=highest, preferred_element_type=jnp.float32
    )


def solve_normal(rows, gram_b, gram_c):
    columns = []
    for member in range(rows.shape[1]):
        normal_mat = gram_b[member] * gram_c[member]
        factor_l = jnp.linalg.cholesky(normal_mat)
        right_side = rows[:, member, :].T
        lower_sol = lax.linalg.triangular_solve(factor_l, right_side, left_side=True, lower=True)
        upper_sol = lax.linalg.triangular_solve(
            factor_l, lower_sol, left_side=True, lower=True, transpose_a=True
        )
        columns.append(upper_sol.T)
    return jnp.stack(columns, axis=1)


def shards(tensor, factor_b, factor_c):
    rows_i, rows_j, rows_k = tensor.shape
    starts, col_count = (factor_b.shape[1], factor_b.shape[2])
    width = starts * col_count
    c_block = lax.all_gather(factor_c, "ja", axis=0, tiled=True)
    partial_value = jnp.dot(
        tensor.reshape(rows_i * rows_j, rows_k),
        c_block.reshape(rows_k, width),
        precision=highest,
        preferred_element_type=jnp.float32,
    ).reshape(rows_i, rows_j, width)
    piece = lax.all_gather(factor_b, "ka", axis=0, tiled=True)
    gram_sum = jnp.zeros((starts, col_count, col_count), jnp.float32)
    count = piece.shape[0]
    flat_rows = piece.reshape(count, width)
    mttkrp = jnp.einsum(
        "ijr,jr->ir",
        partial_value,
        flat_rows,
        precision=highest,
        preferred_element_type=jnp.float32,
    )
    mttkrp, gram_rows = (mttkrp, gram_sum)
    gram_b, gram_c = lax.psum((gram_of(factor_b), gram_of(factor_c)), ("ja", "ka"))
    slab_rows = lax.psum_scatter(mttkrp, "ja", scatter_dimension=0, tiled=True)
    owned = lax.psum_scatter(slab_rows, "ka", scatter_dimension=0, tiled=True)
    owned = owned.reshape(owned.shape[0], starts, col_count)
    factor_raw = solve_normal(owned, gram_b, gram_c)
    squares = jnp.sum(factor_raw * factor_raw, axis=0)
    total = lax.psum(squares, ("ia", "ja", "ka"))
    row_total = rows_i * lax.axis_size("ia")
    weights = jnp.sqrt(total / row_total + 1e-06)
    return (factor_raw / weights[None], weights)


def solution(mesh):
    in_specs = (P("ia", "ja", "ka"), P(("ja", "ka"), None, None), P(("ka", "ja"), None, None))
    out_specs = (P(("ia", "ja", "ka"), None, None), P())
    return jax.shard_map(shards, mesh=mesh, in_specs=in_specs, out_specs=out_specs, check_vma=False)
```

profile of v0, /device:TPU:1, one launch (start us, length us, event | category | flops | bytes accessed | tf_op | source)
XLA Modules:
  0.0 503.4 jit_solution(228719153162087754)
XLA Ops:
  7.2 0.0 copy-start
  7.2 0.0 all-reduce.5.cloned.1.call-start
  7.2 2.1 fusion.22
  9.3 2.1 fusion
  11.4 0.0 all-reduce.5.cloned.1.call-update
  11.4 18.7 %all_gather.7 = f32[128,4,96]{2,1,0:T(4,128)S(1)} all-gather(f32[32,4,96]{2,1,0:T(4,128)} %param.9), channel_id=1, replica_groups=mesh['ia'=16,'ja'=8,'ka'=4] {'ka'}, dimensions={0}, use_global_device_ids=true | all-gather | bytes 245760 | tf_op jit(solution)/shard_map/all_gather | solution.py:40
  30.1 22.2 %all_gather.6 = f32[128,4,96]{2,1,0:T(4,128)S(1)} all-gather(f32[16,4,96]{2,1,0:T(4,128)} %param.10), channel_id=1, replica_groups=mesh['ia'=16,'ja'=8,'ka'=4] {'ja'}, dimensions={0}, use_global_device_ids=true | all-gather | bytes 221184 | tf_op jit(solution)/shard_map/all_gather | solution.py:33
  52.3 0.1 copy.51
  52.4 0.1 copy.52
  52.6 0.1 copy.34
  52.7 1.3 dynamic-slice
  54.0 1.3 dynamic-slice.2
  55.9 0.0 copy-done
  55.9 5.5 %multiply_reduce_fusion = f32[384,32]{0,1:T(8,128)S(1)} fusion(f32[384,128]{0,1:T(8,128)S(1)} %copy.52, f32[32,128,128]{2,1,0:T(8,128)S(1)} %copy-done, f32[128,384,1]{0,1,2:T(8,128)S(1)} %bitcast.141), kind=kOutput, calls=%fused_computation | convolution fusion | flops 2419052544 | bytes 2539520 | tf_op jit(solution)/shard_map/dot_general | solution.py:34
  61.4 23.5 %all-reduce = f32[32,384]{1,0:T(8,128)S(1)} all-reduce(f32[32,384]{1,0:T(8,128)S(1)} %bitcast.142), channel_id=2, replica_groups=mesh['ia'=16,'ja'=8,'ka'=4] {'ja'}, use_global_device_ids=true, to_apply=%region_4.0.clone | all-reduce | flops 12288 | bytes 98304
  84.9 9.5 %all-reduce.1 = f32[4,384]{1,0:T(4,128)S(1)} all-reduce(f32[4,384]{1,0:T(4,128)S(1)} %constant_dynamic-slice_fusion), channel_id=3, replica_groups=mesh['ia'=16,'ja'=8,'ka'=4] {'ka'}, use_global_device_ids=true, to_apply=%region_5.0.clone | all-reduce | flops 1536 | bytes 12288
  94.5 0.7 dynamic-slice_reduce_fusion
  95.1 0.1 reshape.87
  95.2 210.4 %all-reduce.5.cloned.1.call-done = (f32[4,96,96]{1,2,0:T(8,128)}, f32[4,96,96]{1,2,0:T(8,128)}) async-done(((f32[4,96,96]{1,2,0:T(8,128)}, f32[4,96,96]{1,2,0:T(8,128)}), (f32[4,96,96]{1,2,0:T(8,128)}, f32[4,96,96]{1,2,0:T(8,128)})) %all-reduce.5.cloned.1.call-update) | async-done | bytes 294928 | tf_op jit(solution)/shard_map/psum | solution.py:52
  305.6 1.0 fusion.24
  306.6 0.1 copy.33
  306.7 0.1 copy.39
  306.8 0.1 copy.38
  306.9 0.1 copy.37
  307.0 1.0 fusion.9
  308.0 8.8 %cholesky.107 = f32[96,96]{1,0:T(8,128)S(1)} custom-call(f32[96,96]{1,0:T(8,128)S(1)} %get-tuple-element.10), custom_call_target="Cholesky" | custom-call | tf_op jit(solution)/shard_map/jit(cholesky)/cholesky | solution.py:19
  316.8 0.6 compare_reduce_fusion
  317.5 0.7 fusion.5
  318.1 7.4 %custom-call.21 = f32[1,96,96]{1,2,0:T(8,128)S(1)} custom-call(f32[1,96,96]{2,1,0:T(8,128)S(1)} %fusion.5), custom_call_target="InvertDiagBlocksLowerTriangular" | custom-call | tf_op jit(solution)/shard_map/triangular_solve/custom-call.2 | solution.py:22
  325.5 0.1 convolution_bitcast_fusion
  325.6 0.2 fusion.11
  325.8 8.8 %cholesky.96 = f32[96,96]{1,0:T(8,128)S(1)} custom-call(f32[96,96]{1,0:T(8,128)S(1)} %get-tuple-element.11), custom_call_target="Cholesky" | custom-call | tf_op jit(solution)/shard_map/jit(cholesky)/cholesky | solution.py:19
  334.7 0.6 compare_reduce_fusion.1
  335.3 0.7 fusion.4
  336.0 7.4 %custom-call.19 = f32[1,96,96]{1,2,0:T(8,128)S(1)} custom-call(f32[1,96,96]{2,1,0:T(8,128)S(1)} %fusion.4), custom_call_target="InvertDiagBlocksLowerTriangular" | custom-call | tf_op jit(solution)/shard_map/triangular_solve/custom-call.2 | solution.py:22
  343.3 0.1 convolution_bitcast_fusion.1
  343.5 0.2 fusion.14
  343.7 8.8 %cholesky.85 = f32[96,96]{1,0:T(8,128)S(1)} custom-call(f32[96,96]{1,0:T(8,128)S(1)} %get-tuple-element.12), custom_call_target="Cholesky" | custom-call | tf_op jit(solution)/shard_map/jit(cholesky)/cholesky | solution.py:19
  352.5 0.6 compare_reduce_fusion.2
  353.1 0.7 fusion.3
  353.8 7.4 %custom-call.17 = f32[1,96,96]{1,2,0:T(8,128)S(1)} custom-call(f32[1,96,96]{2,1,0:T(8,128)S(1)} %fusion.3), custom_call_target="InvertDiagBlocksLowerTriangular" | custom-call | tf_op jit(solution)/shard_map/triangular_solve/custom-call.2 | solution.py:22
  361.2 0.1 convolution_bitcast_fusion.2
  361.3 0.2 fusion.17
  361.5 9.0 %cholesky.74 = f32[96,96]{1,0:T(8,128)S(1)} custom-call(f32[96,96]{1,0:T(8,128)S(1)} %get-tuple-element.9), custom_call_target="Cholesky" | custom-call | tf_op jit(solution)/shard_map/jit(cholesky)/cholesky | solution.py:19
  370.6 0.6 compare_reduce_fusion.3
  371.2 0.7 fusion.2
  371.9 7.4 %custom-call.15 = f32[1,96,96]{1,2,0:T(8,128)S(1)} custom-call(f32[1,96,96]{2,1,0:T(8,128)S(1)} %fusion.2), custom_call_target="InvertDiagBlocksLowerTriangular" | custom-call | tf_op jit(solution)/shard_map/triangular_solve/custom-call.2 | solution.py:22
  379.2 0.1 convolution_bitcast_fusion.3
  379.4 0.2 fusion.20
  379.6 116.4 %psum.23 = f32[4,96]{1,0:T(4,128)S(1)} all-reduce(f32[4,96]{1,0:T(4,128)S(1)} %fusion.36), channel_id=1, replica_groups=mesh['ia'=16,'ja'=8,'ka'=4] {'ia','ja','ka'}, use_global_device_ids=true, to_apply=%region_6.10 | all-reduce | flops 384 | bytes 3072 | tf_op jit(solution)/shard_map/psum | solution.py:58
  496.0 0.6 divide_bitcast_fusion
  (6 shorter events, 0.2 us)
Async XLA Ops:
  7.2 48.7 %copy-start = (f32[32,128,128]{2,1,0:T(8,128)S(1)}, f32[32,128,128]{2,1,0:T(8,128)}, u32[]{:S(2)}) copy-start(f32[32,128,128]{2,1,0:T(8,128)} %param.8) | copy-start | bytes 6291460
  7.2 298.5 %all-reduce.5.cloned.1.call-start = ((), (), s32[]{:S(2)}) async-start(), calls=%async_computation | async-start | bytes 786432 | tf_op jit(solution)/shard_map/psum | solution.py:52
Sparse Core Ops, SparseCore 0:
  11.5 294.0 all-reduce.4
where the time goes:
time: 504 us; the launch traced here: 503 us
  waiting for transfers between devices  210 us (42%)
  blocking collectives  190 us (38%)
  other arithmetic  72.8 us (14%)
  between operations  14.9 us (3%)
  matrix products  11 us (2%)
    psum x1, waiting for transfers between devices, shards(): lax.psum((gram_of(factor_b), gram_of(factor_c)), ('ja', 'ka'))  210 us
    psum x1, blocking collectives, shards(): total = lax.psum(squares, ('ia', 'ja', 'ka'))  116 us
    another operation x12, other arithmetic, solve_normal(): factor_l = jnp.linalg.cholesky(normal_mat)  38.1 us
    unnamed x2, blocking collectives  33 us
    another operation x8, other arithmetic, solve_normal(): lax.linalg.triangular_solve(factor_l, lower_sol, left_side=True, lower=Tr...  32 us
    all_gather x1, blocking collectives, shards(): c_block = lax.all_gather(factor_c, 'ja', axis=0, tiled=True)  22.2 us
    all_gather x1, blocking collectives, shards(): piece = lax.all_gather(factor_b, 'ka', axis=0, tiled=True)  18.7 us
  transfers between devices with their start and end apart: 1, of which 1 were waited for; matrix products, arithmetic and copies ran while one was open for 2% of the time, Pallas kernels for 0%

commit v1 on v0

--- a/solution.py
+++ b/solution.py
@@ -55,7 +55,7 @@
     owned = owned.reshape(owned.shape[0], starts, col_count)
     factor_raw = solve_normal(owned, gram_b, gram_c)
     squares = jnp.sum(factor_raw * factor_raw, axis=0)
-    total = lax.psum(squares, ("ia", "ja", "ka"))
+    total = jnp.sum(lax.all_gather(squares, ("ia", "ja", "ka")), axis=0)
     row_total = rows_i * lax.axis_size("ia")
     weights = jnp.sqrt(total / row_total + 1e-06)
     return (factor_raw / weights[None], weights)

time: 504 us -> 1880 us (3.73)
  the two profiles are of different devices: /device:TPU:1 before, /device:TPU:64 now
where the time goes in v1:
time: 1880 us
  blocking collectives  1560 us (83%)
  waiting for transfers between devices  215 us (11%)
  other arithmetic  73.8 us (4%)
    all_gather x1, blocking collectives, shards(): total = jnp.sum(lax.all_gather(squares, ('ia', 'ja', 'ka')), axis=0)  1480 us
    psum x1, waiting for transfers between devices, shards(): lax.psum((gram_of(factor_b), gram_of(factor_c)), ('ja', 'ka'))  215 us
    unnamed x2, blocking collectives  41.9 us
    another operation x12, other arithmetic, solve_normal(): factor_l = jnp.linalg.cholesky(normal_mat)  38 us
  transfers between devices with their start and end apart: 1, of which 1 were waited for; matrix products, arithmetic and copies ran while one was open for 0% of the time, Pallas kernels for 0%

profile of v1, /device:TPU:64, one launch (start us, length us, event | category | flops | bytes accessed | tf_op | source)
XLA Modules:
  0.0 1882.5 jit_solution(5585434891779839557)
XLA Ops:
  7.2 0.0 copy-start
  7.2 0.0 all-reduce.5.cloned.1.call-start
  7.2 2.2 fusion
  9.4 2.0 fusion.18
  11.4 0.0 all-reduce.5.cloned.1.call-update
  11.4 19.4 %all_gather.11 = f32[128,4,96]{2,1,0:T(4,128)S(1)} all-gather(f32[32,4,96]{2,1,0:T(4,128)} %param.9), channel_id=1, replica_groups=mesh['ia'=16,'ja'=8,'ka'=4] {'ka'}, dimensions={0}, use_global_device_ids=true | all-gather | bytes 245760 | tf_op jit(solution)/shard_map/all_gather | solution.py:40
  30.9 26.6 %all_gather.10 = f32[128,4,96]{2,1,0:T(4,128)S(1)} all-gather(f32[16,4,96]{2,1,0:T(4,128)} %param.10), channel_id=1, replica_groups=mesh['ia'=16,'ja'=8,'ka'=4] {'ja'}, dimensions={0}, use_global_device_ids=true | all-gather | bytes 221184 | tf_op jit(solution)/shard_map/all_gather | solution.py:33
  57.5 1.3 dynamic-slice.2
  58.8 1.3 dynamic-slice
  60.0 0.1 copy.51
  60.1 0.1 copy.52
  60.3 0.1 copy.34
  61.1 0.0 copy-done
  61.1 5.5 multiply_reduce_fusion
  66.6 29.4 %all-reduce = f32[32,384]{1,0:T(8,128)S(1)} all-reduce(f32[32,384]{1,0:T(8,128)S(1)} %bitcast.154), channel_id=2, replica_groups=mesh['ia'=16,'ja'=8,'ka'=4] {'ja'}, use_global_device_ids=true, to_apply=%region_4.0.clone | all-reduce | flops 12288 | bytes 98304
  96.0 12.5 all-reduce.1
  108.6 0.7 dynamic-slice_reduce_fusion
  109.2 0.1 reshape.212
  109.3 214.7 %all-reduce.5.cloned.1.call-done = (f32[4,96,96]{1,2,0:T(8,128)}, f32[4,96,96]{1,2,0:T(8,128)}) async-done(((f32[4,96,96]{1,2,0:T(8,128)}, f32[4,96,96]{1,2,0:T(8,128)}), (f32[4,96,96]{1,2,0:T(8,128)}, f32[4,96,96]{1,2,0:T(8,128)})) %all-reduce.5.cloned.1.call-update) | async-done | bytes 294928 | tf_op jit(solution)/shard_map/psum | solution.py:52
  324.0 1.0 fusion.20
  325.0 0.1 copy.33
  325.1 0.1 copy.39
  325.2 0.1 copy.38
  325.3 0.1 copy.37
  325.4 1.0 fusion.9
  326.4 8.8 cholesky.74
  335.2 0.6 compare_reduce_fusion.3
  335.9 0.7 fusion.2
  336.5 7.4 custom-call.15
  343.9 8.8 cholesky.107
  352.7 0.6 compare_reduce_fusion
  353.3 0.7 fusion.5
  354.0 7.4 custom-call.21
  361.4 8.8 cholesky.96
  370.2 0.6 compare_reduce_fusion.1
  370.8 0.7 fusion.4
  371.5 7.4 custom-call.19
  378.8 9.0 cholesky.85
  387.9 0.6 compare_reduce_fusion.2
  388.5 0.7 fusion.3
  389.2 7.4 custom-call.17
  396.5 0.1 convolution_bitcast_fusion.1
  396.7 0.2 convolution_bitcast_fusion
  396.9 0.2 convolution_bitcast_fusion.3
  397.0 0.2 convolution_bitcast_fusion.2
  397.2 0.2 convolution_bitcast_fusion.5
  397.4 0.2 convolution_bitcast_fusion.4
  397.6 0.2 convolution_bitcast_fusion.7
  397.8 0.2 convolution_bitcast_fusion.6
  398.0 1475.9 %all_gather.12 = f32[512,4,96]{2,1,0:T(4,128)S(1)} all-gather(f32[1,4,96]{2,1,0:T(4,128)S(1)} %fusion.33), channel_id=1, replica_groups=mesh['ia'=16,'ja'=8,'ka'=4] {'ia','ja','ka'}, dimensions={0}, use_global_device_ids=true | all-gather | bytes 787968 | tf_op jit(solution)/shard_map/all_gather | solution.py:58
  1873.9 0.5 reduce_sum.8
  1874.5 0.6 bitcast_multiply_fusion
  1875.0 0.6 fusion.24
  (6 shorter events, 0.2 us)
Async XLA Ops:
  7.2 53.9 %copy-start = (f32[32,128,128]{2,1,0:T(8,128)S(1)}, f32[32,128,128]{2,1,0:T(8,128)}, u32[]{:S(2)}) copy-start(f32[32,128,128]{2,1,0:T(8,128)} %param.8) | copy-start | bytes 6291460
  7.2 316.9 %all-reduce.5.cloned.1.call-start = ((), (), s32[]{:S(2)}) async-start(), calls=%async_computation | async-start | bytes 786432 | tf_op jit(solution)/shard_map/psum | solution.py:52
Sparse Core Ops, SparseCore 0:
  11.6 312.4 all-reduce.4
